TPU v7x, 128 devices: a whole 4x4x4 slice. The times are simulated.
128 devices in a mesh: depth: 8 (over z, y_lo), height: 16 (over x, y_hi, core).
Axes of the slice: x: 4, y: 4 (y_hi: 2, y_lo: 2; y = y_hi * 2 + y_lo), z: 4, core: 2. Of those that a mesh axis runs over, the one named last changes fastest.
Arguments:
- volume: bfloat16 [32, 32, 128, 128], P(None, 'depth', 'height'), may hold values from -6 to 6
- filters_three: bfloat16 [27, 64, 32], replicated, may hold values from -0.21875 to 0.21875
- filters_four: bfloat16 [27, 128, 64], P(None, 'height'), may hold values from -0.15625 to 0.15625
- cotangent: bfloat16 [128, 16, 64, 64], P(None, 'depth', 'height'), may hold values from -6 to 6
Outputs:
- grad_volume: bfloat16 [32, 32, 128, 128], P(None, 'depth', 'height')
- grad_three: float32 [27, 64, 32], replicated
- grad_four: float32 [27, 128, 64], P(None, 'height')
All inputs are finite; a program needn't handle non-finite values.
Results may differ from a plain program's by a relative error of at most 0.023.
Values may be sent and summed in bfloat16 or wider, within the bound.
A program may use at most 256 MiB of HBM per device.

v0:
```python
import math
import jax
import jax.numpy as jnp
from jax import lax
from jax.sharding import PartitionSpec as P

TANH_SCALE = 0.7978845608028654
CUBIC_TERM = 0.044715


def extended_2(x, sides, width):
    for axis, dim in sides:
        size, length = (lax.axis_size(axis), x.shape[dim])
        up = [(i, (i + 1) % size) for i in range(size - 1)]
        down = [(j, i) for i, j in up]
        last = lax.slice_in_dim(x, length - width, length, axis=dim)
        first = lax.slice_in_dim(x, 0, width, axis=dim)
        before = lax.ppermute(last, axis, up)
        after = lax.ppermute(first, axis, down)
        x = jnp.concatenate([before, x, after], axis=dim)
    return x


def gelu_value(values_in):
    inner = jnp.tanh(TANH_SCALE * (values_in + CUBIC_TERM * values_in * values_in * values_in))
    return 0.5 * values_in * (1.0 + inner)


def gelu_slope(values_in):
    inner = jnp.tanh(TANH_SCALE * (values_in + CUBIC_TERM * values_in * values_in * values_in))
    return 0.5 * (1.0 + inner) + 0.5 * values_in * (1.0 - inner * inner) * TANH_SCALE * (
        1.0 + 3.0 * CUBIC_TERM * values_in * values_in
    )


def pad_width(values_in):
    return jnp.pad(values_in, ((0, 0), (0, 0), (0, 0), (1, 1)))


def forward_taps(padded, weights, depth_cells, height_cells, width_cells):
    running = jnp.zeros((weights.shape[1], depth_cells, height_cells, width_cells), jnp.float32)
    for first in range(3):
        for second in range(3):
            for third in range(3):
                window_piece = padded[
                    :,
                    first : first + depth_cells,
                    second : second + height_cells,
                    third : third + width_cells,
                ]
                running = running + jnp.einsum(
                    "oi,idhw->odhw",
                    weights[9 * first + 3 * second + third],
                    window_piece,
                    preferred_element_type=jnp.float32,
                )
    return running


def transpose_taps(padded, weights, depth_cells, height_cells, width_cells):
    running = jnp.zeros((weights.shape[2], depth_cells, height_cells, width_cells), jnp.float32)
    for first in range(3):
        for second in range(3):
            for third in range(3):
                window_piece = padded[
                    :,
                    2 - first : 2 - first + depth_cells,
                    2 - second : 2 - second + height_cells,
                    2 - third : 2 - third + width_cells,
                ]
                running = running + jnp.einsum(
                    "oi,odhw->idhw",
                    weights[9 * first + 3 * second + third],
                    window_piece,
                    preferred_element_type=jnp.float32,
                )
    return running


def weight_taps(delta, padded, depth_cells, height_cells, width_cells):
    collected = []
    for first in range(3):
        for second in range(3):
            for third in range(3):
                window_piece = padded[
                    :,
                    first : first + depth_cells,
                    second : second + height_cells,
                    third : third + width_cells,
                ]
                collected.append(
                    jnp.einsum(
                        "odhw,idhw->oi", delta, window_piece, preferred_element_type=jnp.float32
                    )
                )
    return jnp.stack(collected, axis=0)


def shards(volume, filters_three, filters_four, cotangent):
    channels_in, depth_cells, height_cells, width_cells = volume.shape
    depth_count = lax.axis_size("depth")
    height_count = lax.axis_size("height")
    scale_three = 1.0 / math.sqrt(
        depth_cells * depth_count * height_cells * height_count * width_cells
    )
    scale_four = 1.0 / math.sqrt(
        depth_cells * depth_count // 2 * (height_cells * height_count // 2) * (width_cells // 2)
    )
    half_depth = depth_cells // 2
    half_height = height_cells // 2
    half_width = width_cells // 2
    extended = extended_2(volume, (("depth", 1), ("height", 2)), 1)
    padded = pad_width(extended)
    act_three = forward_taps(padded, filters_three, depth_cells, height_cells, width_cells)
    channels_mid = act_three.shape[0]
    hidden = gelu_value(act_three).reshape(
        channels_mid, half_depth, 2, half_height, 2, half_width, 2
    )
    pooled = (jnp.sum(hidden, axis=(2, 4, 6)) * 0.125).astype(jnp.bfloat16)
    full_bank = lax.all_gather(filters_four, "height", axis=1, tiled=True)
    rimmed = extended_2(pooled, (("depth", 1), ("height", 2)), 1)
    pooled_pad = pad_width(rimmed)
    act_four = forward_taps(pooled_pad, full_bank, half_depth, half_height, half_width)
    delta_four = (cotangent.astype(jnp.float32) * gelu_slope(act_four)).astype(jnp.bfloat16)
    partial_four = weight_taps(delta_four, pooled_pad, half_depth, half_height, half_width)
    depth_summed = lax.psum(partial_four.astype(jnp.bfloat16), "depth")
    grad_four = (
        lax.psum_scatter(depth_summed, "height", scatter_dimension=1, tiled=True).astype(
            jnp.float32
        )
        * scale_four
    )
    delta_rim = extended_2(delta_four, (("depth", 1), ("height", 2)), 1)
    back_pooled = transpose_taps(
        pad_width(delta_rim), full_bank, half_depth, half_height, half_width
    )
    spread = (
        jnp.repeat(jnp.repeat(jnp.repeat(back_pooled, 2, axis=1), 2, axis=2), 2, axis=3) * 0.125
    )
    delta_three = (spread * gelu_slope(act_three)).astype(jnp.bfloat16)
    partial_three = weight_taps(delta_three, padded, depth_cells, height_cells, width_cells)
    grad_three = lax.psum(partial_three, ("depth", "height")) * scale_three
    delta_extended = extended_2(delta_three, (("depth", 1), ("height", 2)), 1)
    grad_volume = transpose_taps(
        pad_width(delta_extended), filters_three, depth_cells, height_cells, width_cells
    ).astype(jnp.bfloat16)
    return (grad_volume, grad_three, grad_four)


def solution(mesh):
    in_specs = (
        P(None, "depth", "height", None),
        P(),
        P(None, "height", None),
        P(None, "depth", "height", None),
    )
    out_specs = (P(None, "depth", "height", None), P(), P(None, "height", None))
    return jax.shard_map(shards, mesh=mesh, in_specs=in_specs, out_specs=out_specs, check_vma=False)
```

profile of v0, /device:TPU:6, one launch (start us, length us, event | category | flops | bytes accessed | tf_op | source)
XLA Modules:
  0.0 348.1 jit_solution(2866375884435285282)
XLA Ops:
  9.0 3.5 %collective-permute-start = (bf16[32,1,8,128]{3,0,2,1:T(8,128)(2,1)S(1)}, bf16[32,1,8,128]{3,0,2,1:T(8,128)(2,1)S(1)}, u32[]{:S(2)}, u32[]{:S(2)}) collective-permute-start(bf16[32,1,8,128]{3,0,2,1:T(8,128)(2,1)S(1)} %copy.321), channel_id=1, source_target_pairs={{0,16},{16,32},{32,48},{48,64},{64,80},{80,96},{96,112},{1,17},{17... | collective-permute-start | bytes 196616 | tf_op jit(solution)/shard_map/ppermute | solution.py:18
  12.5 1.3 collective-permute-start.1
  15.6 3.1 collective-permute-done.1
  18.8 1.9 collective-permute-start.2
  20.7 6.0 %collective-permute-start.3 = (bf16[32,6,1,128]{3,0,2,1:T(8,128)(2,1)S(1)}, bf16[32,6,1,128]{3,0,2,1:T(8,128)(2,1)S(1)}, u32[]{:S(2)}, u32[]{:S(2)}) collective-permute-start(bf16[32,6,1,128]{3,0,2,1:T(8,128)(2,1)S(1)} %get-tuple-element.19), channel_id=1, source_target_pairs={{1,0},{2,1},{3,2},{4,3},{5,4},{6,5},{7,6},{8,7},{9,8},{10,9},{11,1... | collective-permute-start | bytes 147464 | tf_op jit(solution)/shard_map/ppermute | solution.py:19
  27.1 1.4 collective-permute-done.3
  38.3 2.0 add_multiply_fusion
  40.4 1.8 copy.91
  42.2 2.4 reduce_sum.9
  45.6 4.6 %collective-permute-start.4 = (bf16[64,1,4,64]{0,3,2,1:T(8,128)(2,1)S(1)}, bf16[64,1,4,64]{0,3,2,1:T(8,128)(2,1)S(1)}, u32[]{:S(2)}, u32[]{:S(2)}) collective-permute-start(bf16[64,1,4,64]{0,3,2,1:T(8,128)(2,1)S(1)} %get-tuple-element.33), channel_id=1, source_target_pairs={{0,16},{16,32},{32,48},{48,64},{64,80},{80,96},{96,112},{1,17},{17... | collective-permute-start | bytes 98312 | tf_op jit(solution)/shard_map/ppermute | solution.py:18
  50.2 1.3 collective-permute-start.5
  51.5 23.7 %all_gather.3 = bf16[27,128,64]{2,1,0:T(8,128)(2,1)S(1)} all-gather(bf16[27,8,64]{2,1,0:T(8,128)(2,1)S(1)} %copy-done.14), channel_id=1, replica_groups=mesh['depth'=8,'height'=16] {'height'}, dimensions={1}, use_global_device_ids=true | all-gather | bytes 470016 | tf_op jit(solution)/shard_map/all_gather | solution.py:120
  75.2 2.3 collective-permute-start.6
  77.5 5.7 %collective-permute-start.7 = (bf16[64,4,1,64]{0,3,2,1:T(8,128)(2,1)S(1)}, bf16[64,4,1,64]{0,3,2,1:T(8,128)(2,1)S(1)}, u32[]{:S(2)}, u32[]{:S(2)}) collective-permute-start(bf16[64,4,1,64]{0,3,2,1:T(8,128)(2,1)S(1)} %get-tuple-element.25), channel_id=1, source_target_pairs={{1,0},{2,1},{3,2},{4,3},{5,4},{6,5},{7,6},{8,7},{9,8},{10,9},{11,1... | collective-permute-start | bytes 98312 | tf_op jit(solution)/shard_map/ppermute | solution.py:19
  83.4 1.7 collective-permute-done.7
  96.6 4.0 %collective-permute-start.8 = (bf16[128,1,4,64]{0,3,2,1:T(8,128)(2,1)S(1)}, bf16[128,1,4,64]{0,3,2,1:T(8,128)(2,1)S(1)}, u32[]{:S(2)}, u32[]{:S(2)}) collective-permute-start(bf16[128,1,4,64]{0,3,2,1:T(8,128)(2,1)S(1)} %get-tuple-element.31), channel_id=1, source_target_pairs={{0,16},{16,32},{32,48},{48,64},{64,80},{80,96},{96,112},{1,17},{17... | collective-permute-start | bytes 196616 | tf_op jit(solution)/shard_map/ppermute | solution.py:18
  102.9 4.1 %collective-permute-done.9 = bf16[128,1,4,64]{0,3,2,1:T(8,128)(2,1)S(1)} collective-permute-done((bf16[128,1,4,64]{0,3,2,1:T(8,128)(2,1)S(1)}, bf16[128,1,4,64]{0,3,2,1:T(8,128)(2,1)S(1)}, u32[]{:S(2)}, u32[]{:S(2)}) %collective-permute-start.9) | collective-permute-done | bytes 65568 | tf_op jit(solution)/shard_map/ppermute | solution.py:19
  107.1 4.9 %collective-permute-start.11 = (bf16[128,4,1,64]{0,3,2,1:T(8,128)(2,1)S(1)}, bf16[128,4,1,64]{0,3,2,1:T(8,128)(2,1)S(1)}, u32[]{:S(2)}, u32[]{:S(2)}) collective-permute-start(bf16[128,4,1,64]{0,3,2,1:T(8,128)(2,1)S(1)} %get-tuple-element.23), channel_id=1, source_target_pairs={{1,0},{2,1},{3,2},{4,3},{5,4},{6,5},{7,6},{8,7},{9,8},{10,9},{11,1... | collective-permute-start | bytes 196616 | tf_op jit(solution)/shard_map/ppermute | solution.py:19
  112.0 1.9 collective-permute-start.10
  114.2 5.8 %collective-permute-done.10 = bf16[128,4,1,64]{0,3,2,1:T(8,128)(2,1)S(1)} collective-permute-done((bf16[128,4,1,64]{0,3,2,1:T(8,128)(2,1)S(1)}, bf16[128,4,1,64]{0,3,2,1:T(8,128)(2,1)S(1)}, u32[]{:S(2)}, u32[]{:S(2)}) %collective-permute-start.10) | collective-permute-done | bytes 65568 | tf_op jit(solution)/shard_map/ppermute | solution.py:18
  125.5 1.5 broadcast_in_dim.11
  127.0 2.2 copy.120
  129.2 1.9 fusion.210
  140.7 3.3 copy.149
  145.6 4.6 %collective-permute-start.12 = (bf16[64,1,8,128]{3,0,2,1:T(8,128)(2,1)S(1)}, bf16[64,1,8,128]{3,0,2,1:T(8,128)(2,1)S(1)}, u32[]{:S(2)}, u32[]{:S(2)}) collective-permute-start(bf16[64,1,8,128]{3,0,2,1:T(8,128)(2,1)S(1)} %get-tuple-element.16), channel_id=1, source_target_pairs={{0,16},{16,32},{32,48},{48,64},{64,80},{80,96},{96,112},{1,17},{17... | collective-permute-start | bytes 393224 | tf_op jit(solution)/shard_map/ppermute | solution.py:18
  150.1 134.6 %all-reduce.6.cloned.1.call-done = f32[27,64,32]{1,2,0:T(8,128)} async-done(((f32[27,64,32]{1,2,0:T(8,128)}), f32[27,64,32]{1,2,0:T(8,128)}) %all-reduce.6.cloned.1.call-update) | async-done | bytes 221200 | tf_op jit(solution)/shard_map/psum | solution.py:142
  284.7 1.8 broadcast_multiply_fusion
  286.6 1.9 collective-permute-start.14
  288.5 6.3 %collective-permute-start.15 = (bf16[64,6,1,128]{3,0,2,1:T(8,128)(2,1)S(1)}, bf16[64,6,1,128]{3,0,2,1:T(8,128)(2,1)S(1)}, u32[]{:S(2)}, u32[]{:S(2)}) collective-permute-start(bf16[64,6,1,128]{3,0,2,1:T(8,128)(2,1)S(1)} %get-tuple-element.15), channel_id=1, source_target_pairs={{1,0},{2,1},{3,2},{4,3},{5,4},{6,5},{7,6},{8,7},{9,8},{10,9},{11,1... | collective-permute-start | bytes 294920 | tf_op jit(solution)/shard_map/ppermute | solution.py:19
  295.2 1.5 collective-permute-done.15
  297.3 1.8 select_maximum_fusion
  306.6 33.3 %psum.16 = bf16[27,8,64]{2,0,1:T(8,128)(2,1)S(1)} all-reduce(bf16[27,8,64]{2,0,1:T(8,128)(2,1)} %reduce-scatter.2.cloned.1.call-done), channel_id=1, replica_groups=mesh['depth'=8,'height'=16] {'depth'}, use_global_device_ids=true, to_apply=%region_2.3 | all-reduce | flops 13824 | bytes 55296 | tf_op jit(solution)/shard_map/psum | solution.py:126
  (235 shorter events, 53.3 us)
Async XLA Ops:
  8.0 18.7 %copy-start = (bf16[32,4,8,128]{3,2,1,0:T(8,128)(2,1)S(1)}, bf16[32,4,8,128]{3,2,1,0:T(8,128)(2,1)}, u32[]{:S(2)}) copy-start(bf16[32,4,8,128]{3,2,1,0:T(8,128)(2,1)} %param.4) | copy-start | bytes 786436
  8.0 18.7 %copy-start.6 = (bf16[27,64,32]{1,2,0:T(8,128)(2,1)S(1)}, bf16[27,64,32]{1,2,0:T(8,128)(2,1)}, u32[]{:S(2)}) copy-start(bf16[27,64,32]{1,2,0:T(8,128)(2,1)} %param.5) | copy-start | bytes 331780
  8.0 276.7 %all-reduce.6.cloned.1.call-start = ((), (), s32[]{:S(2)}) async-start(), calls=%async_computation.1 | async-start | bytes 884736 | tf_op jit(solution)/shard_map/psum | solution.py:142
  9.0 5.4 %collective-permute-start = (bf16[32,1,8,128]{3,0,2,1:T(8,128)(2,1)S(1)}, bf16[32,1,8,128]{3,0,2,1:T(8,128)(2,1)S(1)}, u32[]{:S(2)}, u32[]{:S(2)}) collective-permute-start(bf16[32,1,8,128]{3,0,2,1:T(8,128)(2,1)S(1)} %copy.321), channel_id=1, source_target_pairs={{0,16},{16,32},{32,48},{48,64},{64,80},{80,96},{96,112},{1,17},{17... | collective-permute-start | bytes 196616 | tf_op jit(solution)/shard_map/ppermute | solution.py:18
  12.5 6.2 %collective-permute-start.1 = (bf16[32,1,8,128]{3,0,2,1:T(8,128)(2,1)S(1)}, bf16[32,1,8,128]{3,0,2,1:T(8,128)(2,1)S(1)}, u32[]{:S(2)}, u32[]{:S(2)}) collective-permute-start(bf16[32,1,8,128]{3,0,2,1:T(8,128)(2,1)S(1)} %copy.322), channel_id=1, source_target_pairs={{16,0},{32,16},{48,32},{64,48},{80,64},{96,80},{112,96},{17,1},{33... | collective-permute-start | bytes 196616 | tf_op jit(solution)/shard_map/ppermute | solution.py:19
  15.6 19.9 %copy-start.4 = (bf16[32,5,8,128]{3,0,2,1:T(8,128)(2,1)}, bf16[32,5,8,128]{3,0,2,1:T(8,128)(2,1)S(1)}, u32[]{:S(2)}) copy-start(bf16[32,5,8,128]{3,0,2,1:T(8,128)(2,1)S(1)} %get-tuple-element.28) | copy-start | bytes 983044
  18.7 19.6 %copy-start.2 = (bf16[32,5,8,128]{3,0,2,1:T(8,128)(2,1)}, bf16[32,5,8,128]{3,0,2,1:T(8,128)(2,1)S(1)}, u32[]{:S(2)}) copy-start(bf16[32,5,8,128]{3,0,2,1:T(8,128)(2,1)S(1)} %get-tuple-element.35) | copy-start | bytes 983044
  18.8 8.3 %collective-permute-start.2 = (bf16[32,6,1,128]{3,0,2,1:T(8,128)(2,1)S(1)}, bf16[32,6,1,128]{3,0,2,1:T(8,128)(2,1)S(1)}, u32[]{:S(2)}, u32[]{:S(2)}) collective-permute-start(bf16[32,6,1,128]{3,0,2,1:T(8,128)(2,1)S(1)} %get-tuple-element.18), channel_id=1, source_target_pairs={{0,1},{1,2},{2,3},{3,4},{4,5},{5,6},{6,7},{7,8},{8,9},{9,10},{10,1... | collective-permute-start | bytes 147464 | tf_op jit(solution)/shard_map/ppermute | solution.py:18
  20.7 7.8 %collective-permute-start.3 = (bf16[32,6,1,128]{3,0,2,1:T(8,128)(2,1)S(1)}, bf16[32,6,1,128]{3,0,2,1:T(8,128)(2,1)S(1)}, u32[]{:S(2)}, u32[]{:S(2)}) collective-permute-start(bf16[32,6,1,128]{3,0,2,1:T(8,128)(2,1)S(1)} %get-tuple-element.19), channel_id=1, source_target_pairs={{1,0},{2,1},{3,2},{4,3},{5,4},{6,5},{7,6},{8,7},{9,8},{10,9},{11,1... | collective-permute-start | bytes 147464 | tf_op jit(solution)/shard_map/ppermute | solution.py:19
  27.1 9.8 %copy-start.10 = (bf16[32,6,1,128]{3,0,2,1:T(8,128)(2,1)}, bf16[32,6,1,128]{3,0,2,1:T(8,128)(2,1)S(1)}, u32[]{:S(2)}) copy-start(bf16[32,6,1,128]{3,0,2,1:T(8,128)(2,1)S(1)} %collective-permute-done.2) | copy-start | bytes 147460
  28.5 9.5 %copy-start.8 = (bf16[32,6,1,128]{3,0,2,1:T(8,128)(2,1)}, bf16[32,6,1,128]{3,0,2,1:T(8,128)(2,1)S(1)}, u32[]{:S(2)}) copy-start(bf16[32,6,1,128]{3,0,2,1:T(8,128)(2,1)S(1)} %collective-permute-done.3) | copy-start | bytes 147460
  42.2 9.3 %copy-start.14 = (bf16[27,8,64]{2,1,0:T(8,128)(2,1)S(1)}, bf16[27,8,64]{2,1,0:T(8,128)(2,1)}, u32[]{:S(2)}) copy-start(bf16[27,8,64]{2,1,0:T(8,128)(2,1)} %param.6) | copy-start | bytes 82948
  45.6 29.6 %collective-permute-start.4 = (bf16[64,1,4,64]{0,3,2,1:T(8,128)(2,1)S(1)}, bf16[64,1,4,64]{0,3,2,1:T(8,128)(2,1)S(1)}, u32[]{:S(2)}, u32[]{:S(2)}) collective-permute-start(bf16[64,1,4,64]{0,3,2,1:T(8,128)(2,1)S(1)} %get-tuple-element.33), channel_id=1, source_target_pairs={{0,16},{16,32},{32,48},{48,64},{64,80},{80,96},{96,112},{1,17},{17... | collective-permute-start | bytes 98312 | tf_op jit(solution)/shard_map/ppermute | solution.py:18
  50.2 25.0 %collective-permute-start.5 = (bf16[64,1,4,64]{0,3,2,1:T(8,128)(2,1)S(1)}, bf16[64,1,4,64]{0,3,2,1:T(8,128)(2,1)S(1)}, u32[]{:S(2)}, u32[]{:S(2)}) collective-permute-start(bf16[64,1,4,64]{0,3,2,1:T(8,128)(2,1)S(1)} %get-tuple-element.34), channel_id=1, source_target_pairs={{16,0},{32,16},{48,32},{64,48},{80,64},{96,80},{112,96},{17,1},{33... | collective-permute-start | bytes 98312 | tf_op jit(solution)/shard_map/ppermute | solution.py:19
  75.2 8.2 %collective-permute-start.6 = (bf16[64,4,1,64]{0,3,2,1:T(8,128)(2,1)S(1)}, bf16[64,4,1,64]{0,3,2,1:T(8,128)(2,1)S(1)}, u32[]{:S(2)}, u32[]{:S(2)}) collective-permute-start(bf16[64,4,1,64]{0,3,2,1:T(8,128)(2,1)S(1)} %get-tuple-element.24), channel_id=1, source_target_pairs={{0,1},{1,2},{2,3},{3,4},{4,5},{5,6},{6,7},{7,8},{8,9},{9,10},{10,1... | collective-permute-start | bytes 98312 | tf_op jit(solution)/shard_map/ppermute | solution.py:18
  77.5 7.6 %collective-permute-start.7 = (bf16[64,4,1,64]{0,3,2,1:T(8,128)(2,1)S(1)}, bf16[64,4,1,64]{0,3,2,1:T(8,128)(2,1)S(1)}, u32[]{:S(2)}, u32[]{:S(2)}) collective-permute-start(bf16[64,4,1,64]{0,3,2,1:T(8,128)(2,1)S(1)} %get-tuple-element.25), channel_id=1, source_target_pairs={{1,0},{2,1},{3,2},{4,3},{5,4},{6,5},{7,6},{8,7},{9,8},{10,9},{11,1... | collective-permute-start | bytes 98312 | tf_op jit(solution)/shard_map/ppermute | solution.py:19
  96.6 6.4 %collective-permute-start.8 = (bf16[128,1,4,64]{0,3,2,1:T(8,128)(2,1)S(1)}, bf16[128,1,4,64]{0,3,2,1:T(8,128)(2,1)S(1)}, u32[]{:S(2)}, u32[]{:S(2)}) collective-permute-start(bf16[128,1,4,64]{0,3,2,1:T(8,128)(2,1)S(1)} %get-tuple-element.31), channel_id=1, source_target_pairs={{0,16},{16,32},{32,48},{48,64},{64,80},{80,96},{96,112},{1,17},{17... | collective-permute-start | bytes 196616 | tf_op jit(solution)/shard_map/ppermute | solution.py:18
  100.5 6.5 %collective-permute-start.9 = (bf16[128,1,4,64]{0,3,2,1:T(8,128)(2,1)S(1)}, bf16[128,1,4,64]{0,3,2,1:T(8,128)(2,1)S(1)}, u32[]{:S(2)}, u32[]{:S(2)}) collective-permute-start(bf16[128,1,4,64]{0,3,2,1:T(8,128)(2,1)S(1)} %get-tuple-element.32), channel_id=1, source_target_pairs={{16,0},{32,16},{48,32},{64,48},{80,64},{96,80},{112,96},{17,1},{33... | collective-permute-start | bytes 196616 | tf_op jit(solution)/shard_map/ppermute | solution.py:19
  107.1 7.1 %collective-permute-start.11 = (bf16[128,4,1,64]{0,3,2,1:T(8,128)(2,1)S(1)}, bf16[128,4,1,64]{0,3,2,1:T(8,128)(2,1)S(1)}, u32[]{:S(2)}, u32[]{:S(2)}) collective-permute-start(bf16[128,4,1,64]{0,3,2,1:T(8,128)(2,1)S(1)} %get-tuple-element.23), channel_id=1, source_target_pairs={{1,0},{2,1},{3,2},{4,3},{5,4},{6,5},{7,6},{8,7},{9,8},{10,9},{11,1... | collective-permute-start | bytes 196616 | tf_op jit(solution)/shard_map/ppermute | solution.py:19
  112.0 8.0 %collective-permute-start.10 = (bf16[128,4,1,64]{0,3,2,1:T(8,128)(2,1)S(1)}, bf16[128,4,1,64]{0,3,2,1:T(8,128)(2,1)S(1)}, u32[]{:S(2)}, u32[]{:S(2)}) collective-permute-start(bf16[128,4,1,64]{0,3,2,1:T(8,128)(2,1)S(1)} %get-tuple-element.22), channel_id=1, source_target_pairs={{0,1},{1,2},{2,3},{3,4},{4,5},{5,6},{6,7},{7,8},{8,9},{9,10},{10,1... | collective-permute-start | bytes 196616 | tf_op jit(solution)/shard_map/ppermute | solution.py:18
  114.1 6.5 %copy-start.13 = (bf16[27,128,64]{1,2,0:T(8,128)(2,1)}, bf16[27,128,64]{1,2,0:T(8,128)(2,1)S(1)}, u32[]{:S(2)}) copy-start(bf16[27,128,64]{1,2,0:T(8,128)(2,1)S(1)} %fusion.126) | copy-start | bytes 1327108
  129.2 2.2 copy-start.11
  131.1 1.1 copy-start.5
  131.6 1.5 copy-start.9
  133.4 1.5 copy-start.1
  136.0 1.5 copy-start.3
  139.0 5.0 %copy-start.7 = (bf16[27,64,32]{1,2,0:T(8,128)(2,1)S(1)}, bf16[27,64,32]{1,2,0:T(8,128)(2,1)}, u32[]{:S(2)}) copy-start(bf16[27,64,32]{1,2,0:T(8,128)(2,1)} %param.5) | copy-start | bytes 331780
  139.8 166.8 %reduce-scatter.2.cloned.1.call-start = ((), (), s32[]{:S(2)}) async-start(), calls=%async_computation.2 | async-start | bytes 1114112 | tf_op jit(solution)/shard_map/reduce_scatter | solution.py:128
  144.3 142.3 %collective-permute-start.13 = (bf16[64,1,8,128]{3,0,2,1:T(8,128)(2,1)S(1)}, bf16[64,1,8,128]{3,0,2,1:T(8,128)(2,1)S(1)}, u32[]{:S(2)}, u32[]{:S(2)}) collective-permute-start(bf16[64,1,8,128]{3,0,2,1:T(8,128)(2,1)S(1)} %get-tuple-element.17), channel_id=1, source_target_pairs={{16,0},{32,16},{48,32},{64,48},{80,64},{96,80},{112,96},{17,1},{33... | collective-permute-start | bytes 393224 | tf_op jit(solution)/shard_map/ppermute | solution.py:19
  145.6 141.0 %collective-permute-start.12 = (bf16[64,1,8,128]{3,0,2,1:T(8,128)(2,1)S(1)}, bf16[64,1,8,128]{3,0,2,1:T(8,128)(2,1)S(1)}, u32[]{:S(2)}, u32[]{:S(2)}) collective-permute-start(bf16[64,1,8,128]{3,0,2,1:T(8,128)(2,1)S(1)} %get-tuple-element.16), channel_id=1, source_target_pairs={{0,16},{16,32},{32,48},{48,64},{64,80},{80,96},{96,112},{1,17},{17... | collective-permute-start | bytes 393224 | tf_op jit(solution)/shard_map/ppermute | solution.py:18
  286.6 8.6 %collective-permute-start.14 = (bf16[64,6,1,128]{3,0,2,1:T(8,128)(2,1)S(1)}, bf16[64,6,1,128]{3,0,2,1:T(8,128)(2,1)S(1)}, u32[]{:S(2)}, u32[]{:S(2)}) collective-permute-start(bf16[64,6,1,128]{3,0,2,1:T(8,128)(2,1)S(1)} %get-tuple-element.14), channel_id=1, source_target_pairs={{0,1},{1,2},{2,3},{3,4},{4,5},{5,6},{6,7},{7,8},{8,9},{9,10},{10,1... | collective-permute-start | bytes 294920 | tf_op jit(solution)/shard_map/ppermute | solution.py:18
  288.5 8.2 %collective-permute-start.15 = (bf16[64,6,1,128]{3,0,2,1:T(8,128)(2,1)S(1)}, bf16[64,6,1,128]{3,0,2,1:T(8,128)(2,1)S(1)}, u32[]{:S(2)}, u32[]{:S(2)}) collective-permute-start(bf16[64,6,1,128]{3,0,2,1:T(8,128)(2,1)S(1)} %get-tuple-element.15), channel_id=1, source_target_pairs={{1,0},{2,1},{3,2},{4,3},{5,4},{6,5},{7,6},{8,7},{9,8},{10,9},{11,1... | collective-permute-start | bytes 294920 | tf_op jit(solution)/shard_map/ppermute | solution.py:19
  (2 other events, 1.7 us)
Sparse Core Ops, SparseCore 0:
  139.9 144.7 all-reduce.5
Sparse Core Ops, SparseCore 1:
  144.6 66.4 reduce-scatter.1
where the time goes:
time: 349 us; the launch traced here: 348 us
  waiting for transfers between devices  154 us (44%)
  blocking collectives  57 us (16%)
  starting transfers between devices  52.8 us (15%)
  matrix products  43.6 us (12%)
  between operations  16.6 us (5%)
  local copies, waits for them, and re-layouts  14.2 us (4%)
  other arithmetic  10.1 us (3%)
    psum x1, waiting for transfers between devices, shards(): grad_three = lax.psum(partial_three, ('depth', 'height')) * scale_three  135 us
    psum x1, blocking collectives, shards(): depth_summed = lax.psum(partial_four.astype(jnp.bfloat16), 'depth')  33.3 us
    ppermute x8, starting transfers between devices, extended_2(): after = lax.ppermute(first, axis, down)  28.1 us
    ppermute x8, starting transfers between devices, extended_2(): before = lax.ppermute(last, axis, up)  24.6 us
    all_gather x1, blocking collectives, shards(): full_bank = lax.all_gather(filters_four, 'height', axis=1, tiled=True)  23.7 us
    dot_general x54, matrix products, forward_taps(): jnp.einsum('oi,idhw->odhw', weights[9 * first + 3 * second + third], wind...  16.9 us
    dot_general x54, matrix products, weight_taps(): jnp.einsum('odhw,idhw->oi', delta, window_piece, preferred_element_type=j...  14.4 us
    dot_general x54, matrix products, transpose_taps(): jnp.einsum('oi,odhw->idhw', weights[9 * first + 3 * second + third], wind...  12.3 us
  transfers between devices with their start and end apart: 18, of which 9 were waited for; matrix products, arithmetic and copies ran while one was open for 5% of the time, Pallas kernels for 0%

commit v1 on v0

--- a/solution.py
+++ b/solution.py
@@ -117,7 +117,10 @@
         channels_mid, half_depth, 2, half_height, 2, half_width, 2
     )
     pooled = (jnp.sum(hidden, axis=(2, 4, 6)) * 0.125).astype(jnp.bfloat16)
-    full_bank = lax.all_gather(filters_four, "height", axis=1, tiled=True)
+    count = lax.axis_size("height")
+    blocks = jnp.stack([filters_four for _ in range(count)])
+    blocks = lax.all_to_all(blocks, "height", split_axis=0, concat_axis=0)
+    full_bank = jnp.concatenate(blocks, axis=1)
     rimmed = extended_2(pooled, (("depth", 1), ("height", 2)), 1)
     pooled_pad = pad_width(rimmed)
     act_four = forward_taps(pooled_pad, full_bank, half_depth, half_height, half_width)

time: 349 us -> 337 us (0.966)
  blocking collectives: 57 us -> 33.3 us
  starting transfers between devices: 52.8 us -> 61.2 us
    all_gather x1 -> x0, blocking collectives: 23.7 us -> none  [shards(): full_bank = lax.all_gather(filters_four, 'height', axis=1, tiled=True)]
    all_to_all x0 -> x1, starting transfers between devices: none -> 8.64 us  [shards(): blocks = lax.all_to_all(blocks, 'height', split_axis=0, concat_axis=0)]
  transfers between devices with their start and end apart: 18 -> 19, of which waited for: 9 -> 10; matrix products, arithmetic and copies ran while one was open for 5% -> 6% of each run, Pallas kernels for 0% -> 0%
where the time goes in v1:
time: 337 us; the launch traced here: 336 us
  waiting for transfers between devices  153 us (45%)
  starting transfers between devices  61.2 us (18%)
  matrix products  44 us (13%)
  blocking collectives  33.3 us (10%)
  local copies, waits for them, and re-layouts  17.1 us (5%)
  between operations  16.7 us (5%)
  other arithmetic  10.5 us (3%)
    psum x1, waiting for transfers between devices, shards(): grad_three = lax.psum(partial_three, ('depth', 'height')) * scale_three  135 us
    psum x1, blocking collectives, shards(): depth_summed = lax.psum(partial_four.astype(jnp.bfloat16), 'depth')  33.3 us
    ppermute x8, starting transfers between devices, extended_2(): after = lax.ppermute(first, axis, down)  28.4 us
    ppermute x8, starting transfers between devices, extended_2(): before = lax.ppermute(last, axis, up)  24.1 us
    dot_general x54, matrix products, forward_taps(): jnp.einsum('oi,idhw->odhw', weights[9 * first + 3 * second + third], wind...  17.3 us
    dot_general x54, matrix products, weight_taps(): jnp.einsum('odhw,idhw->oi', delta, window_piece, preferred_element_type=j...  14.5 us
    dot_general x54, matrix products, transpose_taps(): jnp.einsum('oi,odhw->idhw', weights[9 * first + 3 * second + third], wind...  12.3 us
    ppermute x8, waiting for transfers between devices, extended_2(): after = lax.ppermute(first, axis, down)  10.6 us
  transfers between devices with their start and end apart: 19, of which 10 were waited for; matrix products, arithmetic and copies ran while one was open for 6% of the time, Pallas kernels for 0%

profile of v1, /device:TPU:6, one launch (start us, length us, event | category | flops | bytes accessed | tf_op | source)
XLA Modules:
  0.0 336.0 jit_solution(11852271952811573718)
XLA Ops:
  9.0 3.5 %collective-permute-start = (bf16[32,1,8,128]{3,0,2,1:T(8,128)(2,1)S(1)}, bf16[32,1,8,128]{3,0,2,1:T(8,128)(2,1)S(1)}, u32[]{:S(2)}, u32[]{:S(2)}) collective-permute-start(bf16[32,1,8,128]{3,0,2,1:T(8,128)(2,1)S(1)} %copy.455), channel_id=1, source_target_pairs={{0,16},{16,32},{32,48},{48,64},{64,80},{80,96},{96,112},{1,17},{17... | collective-permute-start | bytes 196616 | tf_op jit(solution)/shard_map/ppermute | solution.py:18
  15.6 3.1 collective-permute-done.1
  18.7 1.9 collective-permute-start.2
  20.6 6.0 %collective-permute-start.3 = (bf16[32,6,1,128]{3,0,2,1:T(8,128)(2,1)S(1)}, bf16[32,6,1,128]{3,0,2,1:T(8,128)(2,1)S(1)}, u32[]{:S(2)}, u32[]{:S(2)}) collective-permute-start(bf16[32,6,1,128]{3,0,2,1:T(8,128)(2,1)S(1)} %get-tuple-element.19), channel_id=1, source_target_pairs={{1,0},{2,1},{3,2},{4,3},{5,4},{6,5},{7,6},{8,7},{9,8},{10,9},{11,1... | collective-permute-start | bytes 147464 | tf_op jit(solution)/shard_map/ppermute | solution.py:19
  27.1 1.4 collective-permute-done.3
  38.3 1.7 add_multiply_fusion
  40.0 2.0 copy.144
  41.9 2.9 reduce_sum.9
  44.9 4.6 %collective-permute-start.4 = (bf16[64,1,4,64]{0,3,2,1:T(8,128)(2,1)S(1)}, bf16[64,1,4,64]{0,3,2,1:T(8,128)(2,1)S(1)}, u32[]{:S(2)}, u32[]{:S(2)}) collective-permute-start(bf16[64,1,4,64]{0,3,2,1:T(8,128)(2,1)S(1)} %get-tuple-element.33), channel_id=1, source_target_pairs={{0,16},{16,32},{32,48},{48,64},{64,80},{80,96},{96,112},{1,17},{17... | collective-permute-start | bytes 98312 | tf_op jit(solution)/shard_map/ppermute | solution.py:18
  51.0 1.3 reshape.215
  52.3 8.6 %all-to-all-start = ((bf16[16,2,6912]{2,1,0:T(2,128)(2,1)}), bf16[16,2,6912]{2,1,0:T(2,128)(2,1)S(1)}, u32[]{:S(2)}, u32[]{:S(2)}) async-start(bf16[16,2,6912]{2,1,0:T(2,128)(2,1)} %reshape.215), calls=%async_computation | async-start | bytes 884736 | tf_op jit(solution)/shard_map/all_to_all | solution.py:122
  61.0 2.1 collective-permute-start.6
  63.1 5.9 %collective-permute-start.7 = (bf16[64,4,1,64]{0,3,2,1:T(8,128)(2,1)S(1)}, bf16[64,4,1,64]{0,3,2,1:T(8,128)(2,1)S(1)}, u32[]{:S(2)}, u32[]{:S(2)}) collective-permute-start(bf16[64,4,1,64]{0,3,2,1:T(8,128)(2,1)S(1)} %get-tuple-element.25), channel_id=1, source_target_pairs={{1,0},{2,1},{3,2},{4,3},{5,4},{6,5},{7,6},{8,7},{9,8},{10,9},{11,1... | collective-permute-start | bytes 98312 | tf_op jit(solution)/shard_map/ppermute | solution.py:19
  69.0 1.8 collective-permute-done.6
  84.8 3.7 %collective-permute-start.8 = (bf16[128,1,4,64]{0,3,2,1:T(8,128)(2,1)S(1)}, bf16[128,1,4,64]{0,3,2,1:T(8,128)(2,1)S(1)}, u32[]{:S(2)}, u32[]{:S(2)}) collective-permute-start(bf16[128,1,4,64]{0,3,2,1:T(8,128)(2,1)S(1)} %get-tuple-element.31), channel_id=1, source_target_pairs={{0,16},{16,32},{32,48},{48,64},{64,80},{80,96},{96,112},{1,17},{17... | collective-permute-start | bytes 196616 | tf_op jit(solution)/shard_map/ppermute | solution.py:18
  88.4 1.3 collective-permute-start.9
  90.3 4.5 %collective-permute-done.9 = bf16[128,1,4,64]{0,3,2,1:T(8,128)(2,1)S(1)} collective-permute-done((bf16[128,1,4,64]{0,3,2,1:T(8,128)(2,1)S(1)}, bf16[128,1,4,64]{0,3,2,1:T(8,128)(2,1)S(1)}, u32[]{:S(2)}, u32[]{:S(2)}) %collective-permute-start.9) | collective-permute-done | bytes 65568 | tf_op jit(solution)/shard_map/ppermute | solution.py:19
  94.9 5.0 %collective-permute-start.11 = (bf16[128,4,1,64]{0,3,2,1:T(8,128)(2,1)S(1)}, bf16[128,4,1,64]{0,3,2,1:T(8,128)(2,1)S(1)}, u32[]{:S(2)}, u32[]{:S(2)}) collective-permute-start(bf16[128,4,1,64]{0,3,2,1:T(8,128)(2,1)S(1)} %get-tuple-element.23), channel_id=1, source_target_pairs={{1,0},{2,1},{3,2},{4,3},{5,4},{6,5},{7,6},{8,7},{9,8},{10,9},{11,1... | collective-permute-start | bytes 196616 | tf_op jit(solution)/shard_map/ppermute | solution.py:19
  99.9 1.9 collective-permute-start.10
  102.8 5.1 %collective-permute-done.10 = bf16[128,4,1,64]{0,3,2,1:T(8,128)(2,1)S(1)} collective-permute-done((bf16[128,4,1,64]{0,3,2,1:T(8,128)(2,1)S(1)}, bf16[128,4,1,64]{0,3,2,1:T(8,128)(2,1)S(1)}, u32[]{:S(2)}, u32[]{:S(2)}) %collective-permute-start.10) | collective-permute-done | bytes 65568 | tf_op jit(solution)/shard_map/ppermute | solution.py:18
  113.3 1.5 broadcast_in_dim.11
  114.8 2.2 copy.200
  117.0 1.9 fusion.210
  128.5 3.4 copy.229
  133.4 4.6 %collective-permute-start.12 = (bf16[64,1,8,128]{3,0,2,1:T(8,128)(2,1)S(1)}, bf16[64,1,8,128]{3,0,2,1:T(8,128)(2,1)S(1)}, u32[]{:S(2)}, u32[]{:S(2)}) collective-permute-start(bf16[64,1,8,128]{3,0,2,1:T(8,128)(2,1)S(1)} %get-tuple-element.16), channel_id=1, source_target_pairs={{0,16},{16,32},{32,48},{48,64},{64,80},{80,96},{96,112},{1,17},{17... | collective-permute-start | bytes 393224 | tf_op jit(solution)/shard_map/ppermute | solution.py:18
  138.0 134.7 %all-reduce.6.cloned.1.call-done = f32[27,64,32]{1,2,0:T(8,128)} async-done(((f32[27,64,32]{1,2,0:T(8,128)}), f32[27,64,32]{1,2,0:T(8,128)}) %all-reduce.6.cloned.1.call-update) | async-done | bytes 221200 | tf_op jit(solution)/shard_map/psum | solution.py:145
  272.7 1.8 broadcast_multiply_fusion
  274.5 1.9 collective-permute-start.14
  276.5 6.3 %collective-permute-start.15 = (bf16[64,6,1,128]{3,0,2,1:T(8,128)(2,1)S(1)}, bf16[64,6,1,128]{3,0,2,1:T(8,128)(2,1)S(1)}, u32[]{:S(2)}, u32[]{:S(2)}) collective-permute-start(bf16[64,6,1,128]{3,0,2,1:T(8,128)(2,1)S(1)} %get-tuple-element.15), channel_id=1, source_target_pairs={{1,0},{2,1},{3,2},{4,3},{5,4},{6,5},{7,6},{8,7},{9,8},{10,9},{11,1... | collective-permute-start | bytes 294920 | tf_op jit(solution)/shard_map/ppermute | solution.py:19
  283.2 1.5 collective-permute-done.15
  285.3 1.8 select_maximum_fusion
  294.6 33.3 %psum.16 = bf16[27,8,64]{2,0,1:T(8,128)(2,1)S(1)} all-reduce(bf16[27,8,64]{2,0,1:T(8,128)(2,1)} %reduce-scatter.2.cloned.1.call-done), channel_id=1, replica_groups=mesh['depth'=8,'height'=16] {'depth'}, use_global_device_ids=true, to_apply=%region_2.3 | all-reduce | flops 13824 | bytes 55296 | tf_op jit(solution)/shard_map/psum | solution.py:129
  (245 shorter events, 56.2 us)
Async XLA Ops:
  8.0 18.7 %copy-start = (bf16[32,4,8,128]{3,2,1,0:T(8,128)(2,1)S(1)}, bf16[32,4,8,128]{3,2,1,0:T(8,128)(2,1)}, u32[]{:S(2)}) copy-start(bf16[32,4,8,128]{3,2,1,0:T(8,128)(2,1)} %param.4) | copy-start | bytes 786436
  8.0 18.7 %copy-start.7 = (bf16[27,64,32]{1,2,0:T(8,128)(2,1)S(1)}, bf16[27,64,32]{1,2,0:T(8,128)(2,1)}, u32[]{:S(2)}) copy-start(bf16[27,64,32]{1,2,0:T(8,128)(2,1)} %param.5) | copy-start | bytes 331780
  9.0 5.4 %collective-permute-start = (bf16[32,1,8,128]{3,0,2,1:T(8,128)(2,1)S(1)}, bf16[32,1,8,128]{3,0,2,1:T(8,128)(2,1)S(1)}, u32[]{:S(2)}, u32[]{:S(2)}) collective-permute-start(bf16[32,1,8,128]{3,0,2,1:T(8,128)(2,1)S(1)} %copy.455), channel_id=1, source_target_pairs={{0,16},{16,32},{32,48},{48,64},{64,80},{80,96},{96,112},{1,17},{17... | collective-permute-start | bytes 196616 | tf_op jit(solution)/shard_map/ppermute | solution.py:18
  12.5 6.2 %collective-permute-start.1 = (bf16[32,1,8,128]{3,0,2,1:T(8,128)(2,1)S(1)}, bf16[32,1,8,128]{3,0,2,1:T(8,128)(2,1)S(1)}, u32[]{:S(2)}, u32[]{:S(2)}) collective-permute-start(bf16[32,1,8,128]{3,0,2,1:T(8,128)(2,1)S(1)} %copy.456), channel_id=1, source_target_pairs={{16,0},{32,16},{48,32},{64,48},{80,64},{96,80},{112,96},{17,1},{33... | collective-permute-start | bytes 196616 | tf_op jit(solution)/shard_map/ppermute | solution.py:19
  15.5 19.9 %copy-start.4 = (bf16[32,5,8,128]{3,0,2,1:T(8,128)(2,1)}, bf16[32,5,8,128]{3,0,2,1:T(8,128)(2,1)S(1)}, u32[]{:S(2)}) copy-start(bf16[32,5,8,128]{3,0,2,1:T(8,128)(2,1)S(1)} %get-tuple-element.28) | copy-start | bytes 983044
  18.7 19.6 %copy-start.2 = (bf16[32,5,8,128]{3,0,2,1:T(8,128)(2,1)}, bf16[32,5,8,128]{3,0,2,1:T(8,128)(2,1)S(1)}, u32[]{:S(2)}) copy-start(bf16[32,5,8,128]{3,0,2,1:T(8,128)(2,1)S(1)} %get-tuple-element.35) | copy-start | bytes 983044
  18.7 8.3 %collective-permute-start.2 = (bf16[32,6,1,128]{3,0,2,1:T(8,128)(2,1)S(1)}, bf16[32,6,1,128]{3,0,2,1:T(8,128)(2,1)S(1)}, u32[]{:S(2)}, u32[]{:S(2)}) collective-permute-start(bf16[32,6,1,128]{3,0,2,1:T(8,128)(2,1)S(1)} %get-tuple-element.18), channel_id=1, source_target_pairs={{0,1},{1,2},{2,3},{3,4},{4,5},{5,6},{6,7},{7,8},{8,9},{9,10},{10,1... | collective-permute-start | bytes 147464 | tf_op jit(solution)/shard_map/ppermute | solution.py:18
  20.6 7.8 %collective-permute-start.3 = (bf16[32,6,1,128]{3,0,2,1:T(8,128)(2,1)S(1)}, bf16[32,6,1,128]{3,0,2,1:T(8,128)(2,1)S(1)}, u32[]{:S(2)}, u32[]{:S(2)}) collective-permute-start(bf16[32,6,1,128]{3,0,2,1:T(8,128)(2,1)S(1)} %get-tuple-element.19), channel_id=1, source_target_pairs={{1,0},{2,1},{3,2},{4,3},{5,4},{6,5},{7,6},{8,7},{9,8},{10,9},{11,1... | collective-permute-start | bytes 147464 | tf_op jit(solution)/shard_map/ppermute | solution.py:19
  27.0 9.8 %copy-start.11 = (bf16[32,6,1,128]{3,0,2,1:T(8,128)(2,1)}, bf16[32,6,1,128]{3,0,2,1:T(8,128)(2,1)S(1)}, u32[]{:S(2)}) copy-start(bf16[32,6,1,128]{3,0,2,1:T(8,128)(2,1)S(1)} %collective-permute-done.2) | copy-start | bytes 147460
  28.4 9.5 %copy-start.9 = (bf16[32,6,1,128]{3,0,2,1:T(8,128)(2,1)}, bf16[32,6,1,128]{3,0,2,1:T(8,128)(2,1)S(1)}, u32[]{:S(2)}) copy-start(bf16[32,6,1,128]{3,0,2,1:T(8,128)(2,1)S(1)} %collective-permute-done.3) | copy-start | bytes 147460
  41.9 8.9 %copy-start.17 = (bf16[27,8,64]{2,1,0:T(8,128)(2,1)S(1)}, bf16[27,8,64]{2,1,0:T(8,128)(2,1)}, u32[]{:S(2)}) copy-start(bf16[27,8,64]{2,1,0:T(8,128)(2,1)} %param.6) | copy-start | bytes 82948
  44.9 16.0 %collective-permute-start.4 = (bf16[64,1,4,64]{0,3,2,1:T(8,128)(2,1)S(1)}, bf16[64,1,4,64]{0,3,2,1:T(8,128)(2,1)S(1)}, u32[]{:S(2)}, u32[]{:S(2)}) collective-permute-start(bf16[64,1,4,64]{0,3,2,1:T(8,128)(2,1)S(1)} %get-tuple-element.33), channel_id=1, source_target_pairs={{0,16},{16,32},{32,48},{48,64},{64,80},{80,96},{96,112},{1,17},{17... | collective-permute-start | bytes 98312 | tf_op jit(solution)/shard_map/ppermute | solution.py:18
  49.5 11.4 %collective-permute-start.5 = (bf16[64,1,4,64]{0,3,2,1:T(8,128)(2,1)S(1)}, bf16[64,1,4,64]{0,3,2,1:T(8,128)(2,1)S(1)}, u32[]{:S(2)}, u32[]{:S(2)}) collective-permute-start(bf16[64,1,4,64]{0,3,2,1:T(8,128)(2,1)S(1)} %get-tuple-element.34), channel_id=1, source_target_pairs={{16,0},{32,16},{48,32},{64,48},{80,64},{96,80},{112,96},{17,1},{33... | collective-permute-start | bytes 98312 | tf_op jit(solution)/shard_map/ppermute | solution.py:19
  52.3 19.7 %all-to-all-start = ((bf16[16,2,6912]{2,1,0:T(2,128)(2,1)}), bf16[16,2,6912]{2,1,0:T(2,128)(2,1)S(1)}, u32[]{:S(2)}, u32[]{:S(2)}) async-start(bf16[16,2,6912]{2,1,0:T(2,128)(2,1)} %reshape.215), calls=%async_computation | async-start | bytes 884736 | tf_op jit(solution)/shard_map/all_to_all | solution.py:122
  60.9 211.8 %all-reduce.6.cloned.1.call-start = ((), (), s32[]{:S(2)}) async-start(), calls=%async_computation.2 | async-start | bytes 884736 | tf_op jit(solution)/shard_map/psum | solution.py:145
  61.0 9.8 %collective-permute-start.6 = (bf16[64,4,1,64]{0,3,2,1:T(8,128)(2,1)S(1)}, bf16[64,4,1,64]{0,3,2,1:T(8,128)(2,1)S(1)}, u32[]{:S(2)}, u32[]{:S(2)}) collective-permute-start(bf16[64,4,1,64]{0,3,2,1:T(8,128)(2,1)S(1)} %get-tuple-element.24), channel_id=1, source_target_pairs={{0,1},{1,2},{2,3},{3,4},{4,5},{5,6},{6,7},{7,8},{8,9},{9,10},{10,1... | collective-permute-start | bytes 98312 | tf_op jit(solution)/shard_map/ppermute | solution.py:18
  63.1 7.8 %collective-permute-start.7 = (bf16[64,4,1,64]{0,3,2,1:T(8,128)(2,1)S(1)}, bf16[64,4,1,64]{0,3,2,1:T(8,128)(2,1)S(1)}, u32[]{:S(2)}, u32[]{:S(2)}) collective-permute-start(bf16[64,4,1,64]{0,3,2,1:T(8,128)(2,1)S(1)} %get-tuple-element.25), channel_id=1, source_target_pairs={{1,0},{2,1},{3,2},{4,3},{5,4},{6,5},{7,6},{8,7},{9,8},{10,9},{11,1... | collective-permute-start | bytes 98312 | tf_op jit(solution)/shard_map/ppermute | solution.py:19
  70.9 6.4 %copy-start.6 = (bf16[64,4,1,64]{0,3,2,1:T(8,128)(2,1)}, bf16[64,4,1,64]{0,3,2,1:T(8,128)(2,1)S(1)}, u32[]{:S(2)}) copy-start(bf16[64,4,1,64]{0,3,2,1:T(8,128)(2,1)S(1)} %collective-permute-done.7) | copy-start | bytes 98308
  77.6 2.0 copy-start.16
  79.1 1.8 copy-start.15
  84.8 5.6 %collective-permute-start.8 = (bf16[128,1,4,64]{0,3,2,1:T(8,128)(2,1)S(1)}, bf16[128,1,4,64]{0,3,2,1:T(8,128)(2,1)S(1)}, u32[]{:S(2)}, u32[]{:S(2)}) collective-permute-start(bf16[128,1,4,64]{0,3,2,1:T(8,128)(2,1)S(1)} %get-tuple-element.31), channel_id=1, source_target_pairs={{0,16},{16,32},{32,48},{48,64},{64,80},{80,96},{96,112},{1,17},{17... | collective-permute-start | bytes 196616 | tf_op jit(solution)/shard_map/ppermute | solution.py:18
  88.4 6.4 %collective-permute-start.9 = (bf16[128,1,4,64]{0,3,2,1:T(8,128)(2,1)S(1)}, bf16[128,1,4,64]{0,3,2,1:T(8,128)(2,1)S(1)}, u32[]{:S(2)}, u32[]{:S(2)}) collective-permute-start(bf16[128,1,4,64]{0,3,2,1:T(8,128)(2,1)S(1)} %get-tuple-element.32), channel_id=1, source_target_pairs={{16,0},{32,16},{48,32},{64,48},{80,64},{96,80},{112,96},{17,1},{33... | collective-permute-start | bytes 196616 | tf_op jit(solution)/shard_map/ppermute | solution.py:19
  94.9 7.2 %collective-permute-start.11 = (bf16[128,4,1,64]{0,3,2,1:T(8,128)(2,1)S(1)}, bf16[128,4,1,64]{0,3,2,1:T(8,128)(2,1)S(1)}, u32[]{:S(2)}, u32[]{:S(2)}) collective-permute-start(bf16[128,4,1,64]{0,3,2,1:T(8,128)(2,1)S(1)} %get-tuple-element.23), channel_id=1, source_target_pairs={{1,0},{2,1},{3,2},{4,3},{5,4},{6,5},{7,6},{8,7},{9,8},{10,9},{11,1... | collective-permute-start | bytes 196616 | tf_op jit(solution)/shard_map/ppermute | solution.py:19
  99.9 8.0 %collective-permute-start.10 = (bf16[128,4,1,64]{0,3,2,1:T(8,128)(2,1)S(1)}, bf16[128,4,1,64]{0,3,2,1:T(8,128)(2,1)S(1)}, u32[]{:S(2)}, u32[]{:S(2)}) collective-permute-start(bf16[128,4,1,64]{0,3,2,1:T(8,128)(2,1)S(1)} %get-tuple-element.22), channel_id=1, source_target_pairs={{0,1},{1,2},{2,3},{3,4},{4,5},{5,6},{6,7},{7,8},{8,9},{9,10},{10,1... | collective-permute-start | bytes 196616 | tf_op jit(solution)/shard_map/ppermute | solution.py:18
  117.0 2.2 copy-start.12
  119.5 1.5 copy-start.10
  126.8 5.1 %copy-start.8 = (bf16[27,64,32]{1,2,0:T(8,128)(2,1)S(1)}, bf16[27,64,32]{1,2,0:T(8,128)(2,1)}, u32[]{:S(2)}) copy-start(bf16[27,64,32]{1,2,0:T(8,128)(2,1)} %param.5) | copy-start | bytes 331780
  127.6 166.9 %reduce-scatter.2.cloned.1.call-start = ((), (), s32[]{:S(2)}) async-start(), calls=%async_computation.3 | async-start | bytes 1114112 | tf_op jit(solution)/shard_map/reduce_scatter | solution.py:131
  132.1 142.4 %collective-permute-start.13 = (bf16[64,1,8,128]{3,0,2,1:T(8,128)(2,1)S(1)}, bf16[64,1,8,128]{3,0,2,1:T(8,128)(2,1)S(1)}, u32[]{:S(2)}, u32[]{:S(2)}) collective-permute-start(bf16[64,1,8,128]{3,0,2,1:T(8,128)(2,1)S(1)} %get-tuple-element.17), channel_id=1, source_target_pairs={{16,0},{32,16},{48,32},{64,48},{80,64},{96,80},{112,96},{17,1},{33... | collective-permute-start | bytes 393224 | tf_op jit(solution)/shard_map/ppermute | solution.py:19
  133.4 141.1 %collective-permute-start.12 = (bf16[64,1,8,128]{3,0,2,1:T(8,128)(2,1)S(1)}, bf16[64,1,8,128]{3,0,2,1:T(8,128)(2,1)S(1)}, u32[]{:S(2)}, u32[]{:S(2)}) collective-permute-start(bf16[64,1,8,128]{3,0,2,1:T(8,128)(2,1)S(1)} %get-tuple-element.16), channel_id=1, source_target_pairs={{0,16},{16,32},{32,48},{48,64},{64,80},{80,96},{96,112},{1,17},{17... | collective-permute-start | bytes 393224 | tf_op jit(solution)/shard_map/ppermute | solution.py:18
  274.5 8.6 %collective-permute-start.14 = (bf16[64,6,1,128]{3,0,2,1:T(8,128)(2,1)S(1)}, bf16[64,6,1,128]{3,0,2,1:T(8,128)(2,1)S(1)}, u32[]{:S(2)}, u32[]{:S(2)}) collective-permute-start(bf16[64,6,1,128]{3,0,2,1:T(8,128)(2,1)S(1)} %get-tuple-element.14), channel_id=1, source_target_pairs={{0,1},{1,2},{2,3},{3,4},{4,5},{5,6},{6,7},{7,8},{8,9},{9,10},{10,1... | collective-permute-start | bytes 294920 | tf_op jit(solution)/shard_map/ppermute | solution.py:18
  276.5 8.2 %collective-permute-start.15 = (bf16[64,6,1,128]{3,0,2,1:T(8,128)(2,1)S(1)}, bf16[64,6,1,128]{3,0,2,1:T(8,128)(2,1)S(1)}, u32[]{:S(2)}, u32[]{:S(2)}) collective-permute-start(bf16[64,6,1,128]{3,0,2,1:T(8,128)(2,1)S(1)} %get-tuple-element.15), channel_id=1, source_target_pairs={{1,0},{2,1},{3,2},{4,3},{5,4},{6,5},{7,6},{8,7},{9,8},{10,9},{11,1... | collective-permute-start | bytes 294920 | tf_op jit(solution)/shard_map/ppermute | solution.py:19
  (6 other events, 6.5 us)
Sparse Core Ops, SparseCore 0:
  127.8 144.8 all-reduce.5
Sparse Core Ops, SparseCore 1:
  132.4 66.5 reduce-scatter.1
